TPU v7x, 512 devices: a whole 4x8x8 slice. The times are simulated.
512 devices in a mesh: span: 32 (over x, y), seq: 16 (over z, core).
Axes of the slice: x: 4, y: 8, z: 8, core: 2. Of those that a mesh axis runs over, the one named last changes fastest.
Arguments:
- q_tok: bfloat16 [65536, 2048], P(('span', 'seq')), may hold values from -300 to 300
- keys: bfloat16 [65536, 512], P(('span', 'seq')), may hold values from -6 to 6
- values: bfloat16 [65536, 512], P(('span', 'seq')), may hold values from -6 to 6
- beacon_q: bfloat16 [8192, 2048], P(('span', 'seq')), may hold values from -15 to 15
- beacon_k: bfloat16 [8192, 512], P(('span', 'seq')), may hold values from -5 to 5
- beacon_v: bfloat16 [8192, 512], P(('span', 'seq')), may hold values from -6 to 6
- beacon_pos: int32 [8192], P('span'), may hold values from 0 to 2047, as said below
- visible: int32 [32, 32], replicated, may hold values 0 or 1
Outputs:
- out_tok: bfloat16 [65536, 2048], P(('span', 'seq'))
- out_beacon: bfloat16 [8192, 2048], P(('span', 'seq'))
Inputs may be any that keep to these rules, and one draw needn't show every extreme that they name: `beacon_pos`: beacon b of a span stands after raw token 8 * b + r of that span, r from 0 to 7; the first beacon of every span at 0, the last at 2047.
All inputs are finite; a program needn't handle non-finite values.
Results may differ from a plain program's by a relative error of at most 0.005.
Values may be sent and summed in bfloat16 or wider, within the bound.
No kernel may reach another device: no remote copies, remote signals or barrier semaphores. Data moves between devices by JAX's collectives and lax.ppermute only.
A program may use at most 64 MiB of HBM per device.

v0:
```python
import jax
import jax.numpy as jnp
from jax import lax
from jax.sharding import PartitionSpec as P

HD = 128
KVH = 4
QH = 16


masked_score = -1e30


def attend(running, asked, key_block, value_block, allowed):
    run_max, run_sum, run_acc = running
    temper = HD ** (-0.5)
    scores = (
        jnp.einsum("qhd,kd->qhk", asked, key_block, preferred_element_type=jnp.float32) * temper
    )
    masking = allowed[:, None, :]
    scores = jnp.where(masking, scores, masked_score)
    new_max = jnp.maximum(run_max, jnp.max(scores, axis=2))
    weights = jnp.where(masking, jnp.exp(scores - new_max[:, :, None]), 0.0)
    factor = jnp.exp(run_max - new_max)
    new_sum = run_sum * factor + jnp.sum(weights, axis=2)
    mixed = jnp.einsum(
        "qhk,kd->qhd", weights.astype(jnp.bfloat16), value_block, preferred_element_type=jnp.float32
    )
    new_acc = run_acc * factor[:, :, None] + mixed
    return (new_max, new_sum, new_acc)


def on_device(q_tok, keys, values, beacon_q, beacon_k, beacon_v, beacon_pos, visible):
    seq_count = lax.axis_size("seq")
    tok_rows = q_tok.shape[0]
    bea_rows = beacon_q.shape[0]
    all_rows = tok_rows + bea_rows
    heads_here = QH // seq_count
    head_width = heads_here * HD
    kv_head = lax.axis_index("seq") * KVH // seq_count
    my_span = lax.axis_index("span")
    visible_row = visible[my_span]
    queries = jnp.concatenate([q_tok, beacon_q], axis=0).reshape(all_rows, seq_count, head_width)
    key_rows = jnp.concatenate([keys, beacon_k], axis=0)
    value_rows = jnp.concatenate([values, beacon_v], axis=0)
    arrived_q = lax.all_to_all(queries, "seq", split_axis=1, concat_axis=0, tiled=True)
    stacked = jnp.stack([key_rows, value_rows])
    gathered = lax.all_gather(stacked, "seq", axis=1, tiled=True)
    picked = lax.dynamic_slice_in_dim(gathered, kv_head * HD, HD, 2).reshape(
        2, seq_count, all_rows, HD
    )
    own_keys = picked[0]
    own_values = picked[1]
    span_len = seq_count * tok_rows
    beacon_len = seq_count * bea_rows
    total_rows = span_len + beacon_len
    arrived_q = arrived_q.reshape(seq_count, all_rows, heads_here, HD)
    asked = jnp.concatenate(
        [
            arrived_q[:, :tok_rows].reshape(span_len, heads_here, HD),
            arrived_q[:, tok_rows:].reshape(beacon_len, heads_here, HD),
        ],
        axis=0,
    )
    raw_keys = own_keys[:, :tok_rows].reshape(span_len, HD)
    raw_values = own_values[:, :tok_rows].reshape(span_len, HD)
    bea_keys = own_keys[:, tok_rows:].reshape(beacon_len, HD)
    bea_values = own_values[:, tok_rows:].reshape(beacon_len, HD)
    where_at = jnp.concatenate([jnp.arange(span_len, dtype=jnp.int32), beacon_pos])
    beacon_rank = jnp.concatenate(
        [jnp.full((span_len,), -1, jnp.int32), jnp.arange(beacon_len, dtype=jnp.int32)]
    )
    running = (
        jnp.full((total_rows, heads_here), masked_score, jnp.float32),
        jnp.zeros((total_rows, heads_here), jnp.float32),
        jnp.zeros((total_rows, heads_here, HD), jnp.float32),
    )
    group_tiles = 1
    for divisor in range(1, seq_count + 1):
        if seq_count % divisor == 0 and tok_rows * divisor <= max(512, tok_rows):
            group_tiles = divisor
    block_len = tok_rows * group_tiles
    block_count = span_len // block_len
    key_blocks = raw_keys.reshape(block_count, block_len, HD)
    value_blocks = raw_values.reshape(block_count, block_len, HD)
    block_starts = jnp.arange(block_count, dtype=jnp.int32) * block_len

    def raw_step(status, inputs):
        key_block, value_block, first_key = inputs
        allowed = (first_key + jnp.arange(block_len, dtype=jnp.int32))[None, :] <= where_at[:, None]
        return (attend(status, asked, key_block, value_block, allowed), None)

    running, _ = lax.scan(raw_step, running, (key_blocks, value_blocks, block_starts))
    own_allowed = jnp.arange(beacon_len, dtype=jnp.int32)[None, :] <= beacon_rank[:, None]
    running = attend(running, asked, bea_keys, bea_values, own_allowed)
    packed = jnp.stack([bea_keys, bea_values])[None]
    every_span = lax.all_gather(packed, "span", axis=0, tiled=True)
    pair_count = every_span.shape[0] // 2
    paired_keys = every_span[:, 0].reshape(pair_count, 2 * beacon_len, HD)
    paired_values = every_span[:, 1].reshape(pair_count, 2 * beacon_len, HD)

    def prior_step(pair_id, status):
        key_block = lax.dynamic_index_in_dim(paired_keys, pair_id, 0, keepdims=False)
        value_block = lax.dynamic_index_in_dim(paired_values, pair_id, 0, keepdims=False)
        pair_seen = lax.dynamic_slice_in_dim(visible_row, 2 * pair_id, 2)
        pair_spans = 2 * pair_id + jnp.arange(2, dtype=jnp.int32)
        usable = (pair_seen > 0) & (pair_spans < my_span)
        allowed = jnp.repeat(usable, beacon_len)[None, :]
        return attend(status, asked, key_block, value_block, allowed)

    running = lax.fori_loop(0, (my_span + 1) // 2, prior_step, running)
    run_max, run_sum, run_acc = running
    result = (run_acc / run_sum[:, :, None]).astype(jnp.bfloat16)
    raw_out = result[:span_len].reshape(seq_count, tok_rows, head_width)
    bea_out = result[span_len:].reshape(seq_count, bea_rows, head_width)
    returned = lax.all_to_all(
        jnp.concatenate([raw_out, bea_out], axis=1), "seq", split_axis=0, concat_axis=2, tiled=True
    )
    returned = returned.reshape(all_rows, seq_count * head_width)
    return (returned[:tok_rows], returned[tok_rows:])


def solution(mesh):
    return jax.shard_map(
        on_device,
        mesh=mesh,
        in_specs=(
            P(("span", "seq"), None),
            P(("span", "seq"), None),
            P(("span", "seq"), None),
            P(("span", "seq"), None),
            P(("span", "seq"), None),
            P(("span", "seq"), None),
            P("span"),
            P(),
        ),
        out_specs=(P(("span", "seq"), None), P(("span", "seq"), None)),
        check_vma=False,
    )
```

profile of v0, /device:TPU:63, one launch (start us, length us, event | category | flops | bytes accessed | tf_op | source)
XLA Modules:
  0.0 279.6 jit_solution(9790203201025756382)
XLA Ops:
  9.0 2.0 copy_bitcast_fusion
  11.1 11.0 %all-to-all-start = ((bf16[144,16,128]{2,0,1:T(8,128)(2,1)}), bf16[144,16,128]{2,0,1:T(8,128)(2,1)S(1)}, u32[]{:S(2)}, u32[]{:S(2)}) async-start(bf16[144,16,128]{2,0,1:T(8,128)(2,1)} %copy_bitcast_fusion), calls=%async_computation | async-start | bytes 1179648 | tf_op jit(solution)/shard_map/all_to_all | solution.py:46
  22.8 20.2 %all-to-all-done = bf16[144,16,128]{2,0,1:T(8,128)(2,1)S(1)} async-done(((bf16[144,16,128]{2,0,1:T(8,128)(2,1)}), bf16[144,16,128]{2,0,1:T(8,128)(2,1)S(1)}, u32[]{:S(2)}, u32[]{:S(2)}) %all-to-all-start) | async-done | bytes 589856 | tf_op jit(solution)/shard_map/all_to_all | solution.py:46
  43.6 22.9 %all-gather.4.cloned.1.call-done = bf16[2,2304,512]{2,1,0:T(8,128)(2,1)} async-done(((bf16[2,144,512]{2,1,0:T(8,128)(2,1)}), bf16[2,2304,512]{2,1,0:T(8,128)(2,1)}) %all-gather.4.cloned.1.call-update) | async-done | bytes 4718608 | tf_op jit(solution)/shard_map/all_gather | solution.py:48
  70.3 2.0 fusion.52
  72.3 34.0 %while.30 = (s32[]{:T(128)}, f32[2304,1]{0,1:T(1,128)S(1)}, f32[2304,1]{0,1:T(1,128)S(1)}, f32[2304,1,128]{2,0,1:T(8,128)}, s32[4]{0:T(128)}, /*index=5*/s32[230...) while((s32[]{:T(128)}, f32[2304,1]{0,1:T(1,128)S(1)}, ...), condition=%wide.region_3.4_spmd.clone, body=%wide.region_0.3_spmd.clone.sunk | while | flops 619034624 | bytes 26996944 | solution.py:93
  77.4 2.5 fusion.80
  82.8 1.7 fusion.76
  85.9 2.5 fusion.80
  94.4 2.5 fusion.80
  102.9 2.5 fusion.80
  107.7 2.5 fusion.38
  110.3 39.4 %all-gather.6.cloned.1.call-done = bf16[64,256,128]{2,1,0:T(8,128)(2,1)} async-done(((bf16[2,256,128]{2,1,0:T(8,128)(2,1)}), bf16[64,256,128]{2,1,0:T(8,128)(2,1)}) %all-gather.6.cloned.1.call-update) | async-done | bytes 4194320 | tf_op jit(solution)/shard_map/all_gather | solution.py:97
  149.7 4.7 %fusion.51 = (bf16[32,1,256,128]{3,2,1,0:T(8,128)(2,1)}, bf16[32,1,256,128]{3,2,1,0:T(8,128)(2,1)}) fusion(bf16[32,2,256,128]{3,2,1,0:T(8,128)(2,1)} %bitcast.102), kind=kLoop, calls=%fused_computation.86 | loop fusion | bytes 8388608 | tf_op jit(solution)/shard_map/slice | solution.py:100
  154.4 84.9 %while.29 = (s32[]{:T(128)}, f32[2304,1]{0,1:T(1,128)S(1)}, f32[2304,1]{0,1:T(1,128)S(1)}, f32[2304,1,128]{2,0,1:T(8,128)S(1)}, s32[]{:T(128)}, /*index=5*/s32[3...) while((s32[]{:T(128)}, f32[2304,1]{0,1:T(1,128)S(1)}, ...), condition=%wide.region_9.10_spmd, body=%wide.region_6.9_spmd.sunk | while | flops 615193344 | bytes 17527044 | solution.py:111
  157.2 2.4 fusion.73
  162.5 2.4 fusion.73
  167.8 2.4 fusion.73
  173.1 2.4 fusion.73
  178.5 2.4 fusion.73
  183.8 2.4 fusion.73
  189.1 2.4 fusion.73
  194.4 2.4 fusion.73
  199.7 2.4 fusion.73
  205.0 2.4 fusion.73
  210.3 2.4 fusion.73
  215.6 2.4 fusion.73
  220.9 2.4 fusion.73
  226.2 2.4 fusion.73
  231.5 2.4 fusion.73
  236.9 2.4 fusion.73
  239.8 30.4 %all_to_all.30 = bf16[16,144,128]{2,1,0:T(8,128)(2,1)S(1)} all-to-all(bf16[16,144,128]{2,1,0:T(8,128)(2,1)S(1)} %pad_maximum_fusion.1), channel_id=1, replica_groups=mesh['span'=32,'seq'=16] {'seq'}, dimensions={0} | all-to-all | bytes 1179648 | tf_op jit(solution)/shard_map/all_to_all | solution.py:116
  (226 shorter events, 78.2 us)
Async XLA Ops:
  7.2 15.6 %copy-start = (s32[32,32]{1,0:T(8,128)S(1)}, s32[32,32]{1,0:T(8,128)}, u32[]{:S(2)}) copy-start(s32[32,32]{1,0:T(8,128)} %param.19) | copy-start | bytes 12292
  7.2 15.6 %copy-start.11 = (s32[256]{0:T(256)S(1)}, s32[256]{0:T(256)}, u32[]{:S(2)}) copy-start(s32[256]{0:T(256)} %param.18) | copy-start | bytes 3076
  7.2 59.3 %all-gather.4.cloned.1.call-start = ((), (), s32[]{:S(2)}) async-start(), calls=%async_computation.2 | async-start | bytes 5013504 | tf_op jit(solution)/shard_map/all_gather | solution.py:48
  11.1 31.9 %all-to-all-start = ((bf16[144,16,128]{2,0,1:T(8,128)(2,1)}), bf16[144,16,128]{2,0,1:T(8,128)(2,1)S(1)}, u32[]{:S(2)}, u32[]{:S(2)}) async-start(bf16[144,16,128]{2,0,1:T(8,128)(2,1)} %copy_bitcast_fusion), calls=%async_computation | async-start | bytes 1179648 | tf_op jit(solution)/shard_map/all_to_all | solution.py:46
  22.1 127.6 %all-gather.6.cloned.1.call-start = ((), (), s32[]{:S(2)}) async-start(), calls=%async_computation.3 | async-start | bytes 4325376 | tf_op jit(solution)/shard_map/all_gather | solution.py:97
  43.0 0.6 copy-start.7
  43.6 26.7 %copy-start.9 = (s32[2304]{0:T(1024)S(1)}, s32[2304]{0:T(1024)}, u32[]{:S(2)}) copy-start(s32[2304]{0:T(1024)} %constant.92.clone.1) | copy-start | bytes 27652
  68.7 1.6 copy-start.8
  69.6 0.8 copy-start.5
  72.3 34.1 %copy-start.1 = (f32[2304,256]{0,1:T(8,128)}, f32[2304,256]{0,1:T(8,128)S(1)}, u32[]{:S(2)}) copy-start(f32[2304,256]{0,1:T(8,128)S(1)} %get-tuple-element.198) | copy-start | bytes 7077892
  72.3 34.1 %copy-start.10 = (f32[2304]{0:T(1024)S(1)}, f32[2304]{0:T(1024)}, u32[]{:S(2)}) copy-start(f32[2304]{0:T(1024)} %get-tuple-element.197) | copy-start | bytes 27652
  76.1 1.3 copy-start.2
  79.9 1.0 copy-start.3
  84.6 1.3 copy-start.2
  88.4 1.0 copy-start.3
  93.1 1.3 copy-start.2
  96.9 1.0 copy-start.3
  101.6 1.3 copy-start.2
  105.4 1.0 copy-start.3
  106.4 1.3 copy-start.4
  106.4 1.3 copy-start.6
Sparse Core Ops, SparseCore 0:
  10.7 55.7 all-gather.3
  70.4 79.2 all-gather.5
where the time goes:
time: 281 us; the launch traced here: 280 us
  matrix products  88 us (31%)
  waiting for transfers between devices  82.6 us (29%)
  blocking collectives  30.4 us (11%)
  other arithmetic  29.1 us (10%)
  local copies, waits for them, and re-layouts  23 us (8%)
  between operations  14.3 us (5%)
  starting transfers between devices  11.1 us (4%)
    dot_general x21, matrix products, attend(): jnp.einsum('qhk,kd->qhd', weights.astype(jnp.bfloat16), value_block, pref...  51.5 us
    all_gather x1, waiting for transfers between devices, on_device(): every_span = lax.all_gather(packed, 'span', axis=0, tiled=True)  39.4 us
    dot_general x21, matrix products, attend(): jnp.einsum('qhd,kd->qhk', asked, key_block, preferred_element_type=jnp.fl...  36.4 us
    all_to_all x1, blocking collectives, on_device(): lax.all_to_all(jnp.concatenate([raw_out, bea_out], axis=1), 'seq', split_...  30.4 us
    all_gather x1, waiting for transfers between devices, on_device(): gathered = lax.all_gather(stacked, 'seq', axis=1, tiled=True)  22.9 us
    all_to_all x1, waiting for transfers between devices, on_device(): lax.all_to_all(queries, 'seq', split_axis=1, concat_axis=0, tiled=True)  20.2 us
    reduce_sum x21, other arithmetic, attend(): new_sum = run_sum * factor + jnp.sum(weights, axis=2)  17.6 us
    all_to_all x1, starting transfers between devices, on_device(): lax.all_to_all(queries, 'seq', split_axis=1, concat_axis=0, tiled=True)  11 us
  transfers between devices with their start and end apart: 3, of which 3 were waited for; matrix products, arithmetic and copies ran while one was open for 13% of the time, Pallas kernels for 0%

commit v1 on v0

v1 whole, which is shorter than its diff:
```python
import functools

import jax
import jax.numpy as jnp
from jax import lax
from jax.experimental import pallas as pl
from jax.experimental.pallas import tpu as pltpu
from jax.sharding import Mesh, PartitionSpec as P

HD = 128
KVH = 4
QH = 16
GROUP = QH // KVH
NX, NY, NZ, NC = 4, 8, 8, 2
TOK = 128
BEA = 16
HEAD_ROWS = TOK + BEA
TILE = GROUP * HEAD_ROWS
TILES = 4
ROWS = TILES * TILE
HALF = 128
SCALE = HD**-0.5 * 1.4426950408889634
LOWEST = -1e30
CHIPS = ("x", "y", "z", "core")
CONTRACT_LAST = (((1,), (1,)), ((), ()))
VMEM = pl.BlockSpec(memory_space=pltpu.VMEM)
SMEM = pl.BlockSpec(memory_space=pltpu.SMEM)
BF16 = jnp.bfloat16
F32 = jnp.float32


def moves(target):
    pairs = []
    for x in range(NX):
        for y in range(NY):
            for z in range(NZ):
                for core in range(NC):
                    to = target(x, y, z, core)
                    if to is not None:
                        tx, ty, tz, tc = to
                        source = ((x * NY + y) * NZ + z) * NC + core
                        pairs.append((source, ((tx * NY + ty) * NZ + tz % NZ) * NC + tc))
    return pairs


def to_head_group(step):
    return moves(lambda x, y, z, core: (x, y, z + 2 * step, core))


def to_later_x(step):
    return moves(lambda x, y, z, core: (x + step, y, z, core) if x + step < NX else None)


OTHER_CORE = moves(lambda x, y, z, core: (x, y, z, 1 - core))
OTHER_PARITY = moves(lambda x, y, z, core: (x, y, z ^ 1, core))


def kernel_call(body, name, out_shape, in_specs, scratch=(), flops=0, byte_count=0):
    return pl.pallas_call(
        body,
        name=name,
        out_shape=out_shape,
        in_specs=in_specs,
        out_specs=jax.tree.map(lambda _: VMEM, out_shape),
        scratch_shapes=list(scratch),
        compiler_params=pltpu.CompilerParams(vmem_limit_bytes=48 * 2**20),
        cost_estimate=pl.CostEstimate(
            flops=flops, bytes_accessed=byte_count, transcendentals=0
        ),
    )


def pack_beacons(k_ref, v_ref, out_ref):
    for z in range(NZ):
        g = z // 2
        piece = jnp.concatenate(
            [k_ref[:, g * HD : (g + 1) * HD], v_ref[:, g * HD : (g + 1) * HD]], axis=1
        )
        for y in range(NY):
            out_ref[y * NZ + z] = piece


def pack_tokens(place, q_ref, k_ref, v_ref, bq_ref, *outs):
    g = place[2] // 2
    for step in range(TILES):
        dest = lax.rem(g + step, KVH)
        out = outs[step]
        for h in range(GROUP):
            column = pl.multiple_of((dest * GROUP + h) * HD, HD)
            out[h * HEAD_ROWS : h * HEAD_ROWS + TOK, :] = q_ref[:, pl.ds(column, HD)]
            out[h * HEAD_ROWS + TOK : (h + 1) * HEAD_ROWS, :] = bq_ref[:, pl.ds(column, HD)]
        column = pl.multiple_of(dest * HD, HD)
        out[TILE : TILE + TOK, :] = k_ref[:, pl.ds(column, HD)]
        out[TILE + TOK : TILE + 2 * TOK, :] = v_ref[:, pl.ds(column, HD)]


def absorb(state, rows, scores, values, fresh):
    m_ref, l_ref, a_ref = state
    ones = jnp.ones_like(values)
    block_max = jnp.max(scores, axis=1, keepdims=True)
    if fresh:
        new = jnp.broadcast_to(block_max, (scores.shape[0], HD))
    else:
        old = m_ref[rows, :]
        new = jnp.maximum(old, block_max)
    weights = jnp.exp2(scores - new[:, :1]).astype(BF16)
    mixed = jnp.dot(
        weights, jnp.concatenate([values, ones], axis=1), preferred_element_type=F32
    )
    if fresh:
        l_ref[rows, :] = mixed[:, HD:]
        a_ref[rows, :] = mixed[:, :HD]
    else:
        factor = jnp.exp2(old - new)
        l_ref[rows, :] = l_ref[rows, :] * factor + mixed[:, HD:]
        a_ref[rows, :] = a_ref[rows, :] * factor + mixed[:, :HD]
    m_ref[rows, :] = new


def score(asked, keys):
    return lax.dot_general(asked, keys, CONTRACT_LAST, preferred_element_type=F32) * SCALE


def list_visible(place, visible, shifts, chosen):
    my_span = place[0] * NY + place[1]
    count = jnp.int32(0)
    for block, shift in enumerate(shifts):
        first = lax.rem(place[0] + NX - shift, NX) * NY
        for y in range(NY):
            earlier = first + y
            usable = (earlier < my_span) & (visible[my_span, earlier] > 0)

            @pl.when(usable)
            def _():
                chosen[count] = block * NY + y

            count = count + usable.astype(jnp.int32)
    return count


def absorb_prior(count, chosen, q_ref, mine, other, state):
    def block(spans):
        keys = jnp.concatenate([r[s, :, :HD] for s in spans for r in (mine, other)], axis=0)
        values = jnp.concatenate([r[s, :, HD:] for s in spans for r in (mine, other)], axis=0)
        for piece in range(ROWS // HEAD_ROWS):
            rows = slice(piece * HEAD_ROWS, (piece + 1) * HEAD_ROWS)
            tile, h = divmod(piece, GROUP)
            asked = q_ref[tile, h * HEAD_ROWS : (h + 1) * HEAD_ROWS, :]
            absorb(state, rows, score(asked, keys), values, False)

    done = jnp.int32(0)
    for size in (4, 2, 1):

        def step(i, _, size=size, done=done):
            block([chosen[done + size * i + j] for j in range(size)])
            return 0

        turns = (count - done) // size
        lax.fori_loop(0, turns, step, 0)
        done = done + turns * size


def attend_raw(
    place, visible, bpos, q_ref, kv_o, kv_c, kv_z, kv_zc, mine, other, m_ref, l_ref, a_ref, chosen
):
    state = (m_ref, l_ref, a_ref)
    y, z, core = place[1], place[2], place[3]
    g, parity = z // 2, lax.rem(z, 2)
    pieces = (kv_o, kv_c, kv_z, kv_zc)
    here = parity * 256 + core * 128
    lane = lax.broadcasted_iota(jnp.int32, (1, 512), 1)
    combo = lane // 128
    key_at = ((parity ^ (combo // 2)) * 2 + (core ^ (combo % 2))) * 128 + lane % 128
    blane = lax.broadcasted_iota(jnp.int32, (1, 256), 1)
    brow = blane % 128
    beacon_at = (brow // BEA) * 32 + (core ^ (blane // 128)) * BEA + brow % BEA
    raw_rows = lax.broadcasted_iota(jnp.int32, (TOK, 1), 0) + here
    own_keys = jnp.concatenate([mine[y, :, :HD], other[y, :, :HD]], axis=0)
    own_values = jnp.concatenate([mine[y, :, HD:], other[y, :, HD:]], axis=0)

    def tile_step(tile, _):
        source = lax.rem(g - tile + KVH, KVH)
        first = source * 64 + parity * 32 + core * BEA
        at = bpos[pl.ds(pl.multiple_of(first, BEA), BEA), :1] - source * 512
        row_at = jnp.concatenate([raw_rows, at], axis=0)
        rank = first + lax.broadcasted_iota(jnp.int32, (BEA, 1), 0)
        row_rank = jnp.concatenate([jnp.full((TOK, 1), -1, jnp.int32), rank], axis=0)
        keys = jnp.concatenate([r[tile, :TOK, :] for r in pieces] + [own_keys], axis=0)
        values = jnp.concatenate([r[tile, TOK:, :] for r in pieces] + [own_values], axis=0)
        allowed = jnp.concatenate([key_at <= row_at, beacon_at <= row_rank], axis=1)
        base = tile * TILE

        def rows_of(h):
            return pl.ds(pl.multiple_of(base + h * HEAD_ROWS, HEAD_ROWS), HEAD_ROWS)

        for h in range(GROUP):
            asked = q_ref[tile, h * HEAD_ROWS : (h + 1) * HEAD_ROWS, :]
            scores = jnp.where(allowed, score(asked, keys), LOWEST)
            absorb(state, rows_of(h), scores, values, True)

        def earlier_step(e, _):
            there = lax.rem(g - e + KVH, KVH)
            keys = jnp.concatenate([r[there, :TOK, :] for r in pieces], axis=0)
            values = jnp.concatenate([r[there, TOK:, :] for r in pieces], axis=0)
            for h in range(GROUP):
                asked = q_ref[tile, h * HEAD_ROWS : (h + 1) * HEAD_ROWS, :]
                absorb(state, rows_of(h), score(asked, keys), values, False)
            return 0

        lax.fori_loop(0, source, earlier_step, 0)
        return 0

    lax.fori_loop(0, TILES, tile_step, 0)
    count = list_visible(place, visible, (0,), chosen)
    absorb_prior(count, chosen, q_ref, mine, other, state)


def attend_prior(
    shifts, place, visible, q_ref, mine, other, m_in, l_in, a_in, m_ref, l_ref, a_ref, chosen
):
    m_ref[...] = m_in[...]
    l_ref[...] = l_in[...]
    a_ref[...] = a_in[...]
    count = list_visible(place, visible, shifts, chosen)
    absorb_prior(count, chosen, q_ref, mine, other, (m_ref, l_ref, a_ref))


def attend_last(shifts, place, visible, q_ref, mine, other, m_in, l_in, a_in, *rest):
    outs, (m_ref, l_ref, a_ref, chosen) = rest[:TILES], rest[TILES:]
    attend_prior(
        shifts, place, visible, q_ref, mine, other, m_in, l_in, a_in, m_ref, l_ref, a_ref, chosen
    )
    for tile in range(TILES):
        rows = slice(tile * TILE, (tile + 1) * TILE)
        outs[tile][...] = (a_ref[rows, :] / l_ref[rows, :]).astype(BF16)


def unpack_outputs(place, r0, r1, r2, r3, tok_ref, bea_ref):
    g = place[2] // 2
    for step, ref in enumerate((r0, r1, r2, r3)):
        dest = lax.rem(g + step, KVH)
        for h in range(GROUP):
            column = pl.multiple_of((dest * GROUP + h) * HD, HD)
            tok_ref[:, pl.ds(column, HD)] = ref[h * HEAD_ROWS : h * HEAD_ROWS + TOK, :]
            bea_ref[:, pl.ds(column, HD)] = ref[h * HEAD_ROWS + TOK : (h + 1) * HEAD_ROWS, :]


def on_device(q_tok, keys, values, beacon_q, beacon_k, beacon_v, beacon_pos, visible):
    place = jnp.stack([lax.axis_index(a) for a in CHIPS]).astype(jnp.int32)
    to_send = kernel_call(
        pack_beacons,
        "pack_beacons",
        jax.ShapeDtypeStruct((NY * NZ, BEA, 2 * HD), BF16),
        [VMEM] * 2,
        byte_count=600000,
    )(beacon_k, beacon_v)
    arrived = lax.all_to_all(to_send, ("y", "z"), 0, 0, tiled=True)
    block0 = arrived.reshape(NY, HALF, 2 * HD)

    chunks = kernel_call(
        pack_tokens,
        "pack_tokens",
        [jax.ShapeDtypeStruct((TILE + 2 * TOK, HD), BF16)] * TILES,
        [SMEM] + [VMEM] * 4,
        byte_count=1800000,
    )(place, q_tok, keys, values, beacon_q)
    got = [chunks[0]] + [
        lax.ppermute(chunks[step], CHIPS, to_head_group(step)) for step in range(1, TILES)
    ]
    asked = jnp.stack([piece[:TILE] for piece in got])
    kv_o = jnp.stack([piece[TILE:] for piece in got])
    kv_z = lax.ppermute(kv_o, CHIPS, OTHER_PARITY)
    kv_c = lax.ppermute(kv_o, CHIPS, OTHER_CORE)
    kv_zc = lax.ppermute(kv_z, CHIPS, OTHER_CORE)

    from1 = lax.ppermute(block0, CHIPS, to_later_x(1))
    from3 = lax.ppermute(block0, CHIPS, to_later_x(3))
    from2 = lax.ppermute(block0, CHIPS, to_later_x(2))
    block0c = lax.ppermute(block0, CHIPS, OTHER_CORE)
    block13 = jnp.concatenate([from1, from3], axis=0)
    block13c = lax.ppermute(block13, CHIPS, OTHER_CORE)
    block2c = lax.ppermute(from2, CHIPS, OTHER_CORE)

    bpos = jnp.broadcast_to(beacon_pos[:, None], (256, HD))
    state_shape = [jax.ShapeDtypeStruct((ROWS, HD), F32)] * 3
    chosen = pltpu.SMEM((NX * NY,), jnp.int32)
    per_span = ROWS * 256 * HD * 4
    state = kernel_call(
        attend_raw,
        "attend_raw",
        state_shape,
        [SMEM] * 2 + [VMEM] * 8,
        [chosen],
        flops=16 * per_span,
        byte_count=6000000,
    )(place, visible, bpos, asked, kv_o, kv_c, kv_z, kv_zc, block0, block0c)
    state = kernel_call(
        functools.partial(attend_prior, (1, 3)),
        "attend_next",
        state_shape,
        [SMEM] * 2 + [VMEM] * 6,
        [chosen],
        flops=16 * per_span,
        byte_count=9000000,
    )(place, visible, asked, block13, block13c, *state)
    mixed = kernel_call(
        functools.partial(attend_last, (2,)),
        "attend_last",
        [jax.ShapeDtypeStruct((TILE, HD), BF16)] * TILES,
        [SMEM] * 2 + [VMEM] * 6,
        [pltpu.VMEM((ROWS, HD), F32)] * 3 + [chosen],
        flops=8 * per_span,
        byte_count=6000000,
    )(place, visible, asked, from2, block2c, *state)
    back = [mixed[0]] + [
        lax.ppermute(mixed[step], CHIPS, to_head_group(-step)) for step in range(1, TILES)
    ]
    return kernel_call(
        unpack_outputs,
        "unpack_outputs",
        [
            jax.ShapeDtypeStruct((TOK, QH * HD), BF16),
            jax.ShapeDtypeStruct((BEA, QH * HD), BF16),
        ],
        [SMEM] + [VMEM] * 4,
        byte_count=1200000,
    )(place, *back)


def solution(mesh):
    chips = Mesh(mesh.devices.reshape(NX, NY, NZ, NC), CHIPS)
    rows = P(CHIPS, None)
    return jax.shard_map(
        on_device,
        mesh=chips,
        in_specs=(rows, rows, rows, rows, rows, rows, P(("x", "y")), P()),
        out_specs=(rows, rows),
        check_vma=False,
    )
```

time: 281 us -> 163 us (0.58)
  the two profiles are of different devices: /device:TPU:63 before, /device:TPU:94 now
where the time goes in v1:
time: 163 us; the launch traced here: 162 us
  starting transfers between devices  56.9 us (35%)
  waiting for transfers between devices  50.3 us (31%)
  Pallas kernels  49.1 us (30%)
  local copies, waits for them, and re-layouts  5.07 us (3%)
    ppermute x3, waiting for transfers between devices, on_device(): lax.ppermute(chunks[step], CHIPS, to_head_group(step))  17.7 us
    ppermute x3, waiting for transfers between devices, on_device(): lax.ppermute(mixed[step], CHIPS, to_head_group(-step))  17.4 us
    pallas_call x1, Pallas kernels, on_device(): kernel_call(functools.partial(attend_prior, (1, 3)), 'attend_next', state...  17.3 us
    pallas_call x1, Pallas kernels, on_device(): kernel_call(attend_raw, 'attend_raw', state_shape, [SMEM] * 2 + [VMEM] *...  17.2 us
    all_to_all x1, starting transfers between devices, on_device(): arrived = lax.all_to_all(to_send, ('y', 'z'), 0, 0, tiled=True)  15.5 us
    ppermute x1, waiting for transfers between devices, on_device(): from2 = lax.ppermute(block0, CHIPS, to_later_x(2))  13.9 us
    ppermute x3, starting transfers between devices, on_device(): lax.ppermute(chunks[step], CHIPS, to_head_group(step))  13.1 us
    ppermute x3, starting transfers between devices, on_device(): lax.ppermute(mixed[step], CHIPS, to_head_group(-step))  12.4 us
  transfers between devices with their start and end apart: 16, of which 6 were waited for; matrix products, arithmetic and copies ran while one was open for 0% of the time, Pallas kernels for 22%

profile of v1, /device:TPU:94, one launch (start us, length us, event | category | flops | bytes accessed | tf_op | source)
XLA Modules:
  0.0 162.5 jit_solution(13072976403595234634)
XLA Ops:
  0.7 0.8 copy-done.4
  2.2 0.8 pack_beacons.1
  3.0 15.5 %all-to-all-start = ((bf16[64,16,256]{2,1,0:T(8,128)(2,1)}), bf16[64,16,256]{2,1,0:T(8,128)(2,1)S(1)}, u32[]{:S(2)}, u32[]{:S(2)}) async-start(bf16[64,16,256]{2,1,0:T(8,128)(2,1)} %pack_beacons.1), calls=%async_computation | async-start | bytes 1048576 | tf_op jit(solution)/shard_map/all_to_all | solution.py:257
  18.6 0.8 pack_tokens.1
  19.4 4.6 %collective-permute-start.2 = (bf16[832,128]{1,0:T(8,128)(2,1)S(1)}, bf16[832,128]{1,0:T(8,128)(2,1)S(1)}, u32[]{:S(2)}, u32[]{:S(2)}) collective-permute-start(bf16[832,128]{1,0:T(8,128)(2,1)S(1)} %get-tuple-element.19), channel_id=1, source_target_pairs={{0,12},{1,13},{2,14},{3,15},{4,0},{5,1},{6,2},{7,3},{8,4},{9,5},{1... | collective-permute-start | bytes 638984 | tf_op jit(solution)/shard_map/ppermute | solution.py:268
  24.0 5.1 %collective-permute-start.1 = (bf16[832,128]{1,0:T(8,128)(2,1)S(1)}, bf16[832,128]{1,0:T(8,128)(2,1)S(1)}, u32[]{:S(2)}, u32[]{:S(2)}) collective-permute-start(bf16[832,128]{1,0:T(8,128)(2,1)S(1)} %get-tuple-element.18), channel_id=1, source_target_pairs={{0,8},{1,9},{2,10},{3,11},{4,12},{5,13},{6,14},{7,15},{8,0},{9,1},... | collective-permute-start | bytes 638984 | tf_op jit(solution)/shard_map/ppermute | solution.py:268
  29.2 3.4 %collective-permute-start = (bf16[832,128]{1,0:T(8,128)(2,1)S(1)}, bf16[832,128]{1,0:T(8,128)(2,1)S(1)}, u32[]{:S(2)}, u32[]{:S(2)}) collective-permute-start(bf16[832,128]{1,0:T(8,128)(2,1)S(1)} %get-tuple-element.17), channel_id=1, source_target_pairs={{0,4},{1,5},{2,6},{3,7},{4,8},{5,9},{6,10},{7,11},{8,12},{9,13},{1... | collective-permute-start | bytes 638984 | tf_op jit(solution)/shard_map/ppermute | solution.py:268
  32.6 7.9 %collective-permute-done.2 = bf16[832,128]{1,0:T(8,128)(2,1)S(1)} collective-permute-done((bf16[832,128]{1,0:T(8,128)(2,1)S(1)}, bf16[832,128]{1,0:T(8,128)(2,1)S(1)}, u32[]{:S(2)}, u32[]{:S(2)}) %collective-permute-start.2) | collective-permute-done | bytes 213024 | tf_op jit(solution)/shard_map/ppermute | solution.py:268
  40.5 1.3 collective-permute-start.5
  41.8 1.3 collective-permute-start.6
  43.1 9.9 %collective-permute-done.1 = bf16[832,128]{1,0:T(8,128)(2,1)S(1)} collective-permute-done((bf16[832,128]{1,0:T(8,128)(2,1)S(1)}, bf16[832,128]{1,0:T(8,128)(2,1)S(1)}, u32[]{:S(2)}, u32[]{:S(2)}) %collective-permute-start.1) | collective-permute-done | bytes 213024 | tf_op jit(solution)/shard_map/ppermute | solution.py:268
  53.0 1.9 %collective-permute-start.9 = (bf16[4,256,128]{2,1,0:T(8,128)(2,1)S(1)}, bf16[4,256,128]{2,1,0:T(8,128)(2,1)S(1)}, u32[]{:S(2)}, u32[]{:S(2)}) collective-permute-start(bf16[4,256,128]{2,1,0:T(8,128)(2,1)S(1)} %pad_maximum_fusion.1.kv_o), channel_id=1, source_target_pairs={{0,2},{1,3},{2,0},{3,1},{4,6},{5,7},{6,4},{7,5},{8,10},{9,11},{10,... | collective-permute-start | bytes 786440 | tf_op jit(solution)/shard_map/ppermute | solution.py:272
  54.9 1.9 %collective-permute-start.8 = (bf16[4,256,128]{2,1,0:T(8,128)(2,1)S(1)}, bf16[4,256,128]{2,1,0:T(8,128)(2,1)S(1)}, u32[]{:S(2)}, u32[]{:S(2)}) collective-permute-start(bf16[4,256,128]{2,1,0:T(8,128)(2,1)S(1)} %pad_maximum_fusion.1.kv_o), channel_id=1, source_target_pairs={{0,1},{1,0},{2,3},{3,2},{4,5},{5,4},{6,7},{7,6},{8,9},{9,8},{10,11... | collective-permute-start | bytes 786440 | tf_op jit(solution)/shard_map/ppermute | solution.py:273
  56.9 1.2 collective-permute-done.6
  58.2 1.9 %collective-permute-start.7 = (bf16[16,128,256]{2,1,0:T(8,128)(2,1)S(1)}, bf16[16,128,256]{2,1,0:T(8,128)(2,1)S(1)}, u32[]{:S(2)}, u32[]{:S(2)}) collective-permute-start(bf16[16,128,256]{2,1,0:T(8,128)(2,1)S(1)} %constant_dynamic-update-slice_fusion.mine), channel_id=1, source_target_pairs={{0,1},{1,0},{2,3},{3,2},{4,5},{5,4},{6,7},{7,6},{8,9},{9,8},{10,11... | collective-permute-start | bytes 3145736 | tf_op jit(solution)/shard_map/ppermute | solution.py:281
  60.2 2.4 %collective-permute-start.11 = (bf16[8,128,256]{2,1,0:T(8,128)(2,1)S(1)}, bf16[8,128,256]{2,1,0:T(8,128)(2,1)S(1)}, u32[]{:S(2)}, u32[]{:S(2)}) collective-permute-start(bf16[8,128,256]{2,1,0:T(8,128)(2,1)S(1)} %bitcast.23), channel_id=1, source_target_pairs={{0,1},{1,0},{2,3},{3,2},{4,5},{5,4},{6,7},{7,6},{8,9},{9,8},{10,11... | collective-permute-start | bytes 1572872 | tf_op jit(solution)/shard_map/ppermute | solution.py:279
  62.6 1.3 collective-permute-start.3
  63.9 1.9 %collective-permute-start.10 = (bf16[4,256,128]{2,1,0:T(8,128)(2,1)S(1)}, bf16[4,256,128]{2,1,0:T(8,128)(2,1)S(1)}, u32[]{:S(2)}, u32[]{:S(2)}) collective-permute-start(bf16[4,256,128]{2,1,0:T(8,128)(2,1)S(1)} %collective-permute-done.9.kv_z), channel_id=1, source_target_pairs={{0,1},{1,0},{2,3},{3,2},{4,5},{5,4},{6,7},{7,6},{8,9},{9,8},{10,11... | collective-permute-start | bytes 786440 | tf_op jit(solution)/shard_map/ppermute | solution.py:274
  65.9 13.9 %collective-permute-done.3.mine = bf16[8,128,256]{2,1,0:T(8,128)(2,1)S(1)} collective-permute-done((bf16[8,128,256]{2,1,0:T(8,128)(2,1)S(1)}, bf16[8,128,256]{2,1,0:T(8,128)(2,1)S(1)}, u32[]{:S(2)}, u32[]{:S(2)}) %collective-permute-start.3) | collective-permute-done | bytes 524320 | tf_op jit(solution)/shard_map/ppermute | solution.py:278
  79.8 1.9 %collective-permute-start.4 = (bf16[8,128,256]{2,1,0:T(8,128)(2,1)S(1)}, bf16[8,128,256]{2,1,0:T(8,128)(2,1)S(1)}, u32[]{:S(2)}, u32[]{:S(2)}) collective-permute-start(bf16[8,128,256]{2,1,0:T(8,128)(2,1)S(1)} %collective-permute-done.3.mine), channel_id=1, source_target_pairs={{0,1},{1,0},{2,3},{3,2},{4,5},{5,4},{6,7},{7,6},{8,9},{9,8},{10,11... | collective-permute-start | bytes 1572872 | tf_op jit(solution)/shard_map/ppermute | solution.py:282
  81.9 17.2 %attend_raw.1 = (f32[2304,128]{1,0:T(8,128)S(1)}, f32[2304,128]{1,0:T(8,128)S(1)}, f32[2304,128]{1,0:T(8,128)}) custom-call(s32[4]{0:T(128)S(1)} %pad_add_fusion.place, s32[32,32]{1,0:T(8,128)S(1)} %copy-done.6, s32[256,128]{1,0:T(8,128)S(1)} %broadcast_in_dim.2.bpos, bf16[4,576,128]{2,1,0:T(8,128)(2,1)S(1)} %pad_maximum_fusion.q_ref, ...), custom_call_target="tpu_custom_call" | custom-call | flops 4831838208 | bytes 6000000 | tf_op jit(solution)/shard_map/attend_raw/pallas_call | solution.py:288
  99.0 1.0 copy-done.8
  100.1 1.0 copy-done.9
  101.1 17.3 %attend_next.1 = (f32[2304,128]{1,0:T(8,128)S(1)}, f32[2304,128]{1,0:T(8,128)S(1)}, f32[2304,128]{1,0:T(8,128)}) custom-call(s32[4]{0:T(128)S(1)} %pad_add_fusion.place, s32[32,32]{1,0:T(8,128)S(1)} %copy-done.6, bf16[4,576,128]{2,1,0:T(8,128)(2,1)S(1)} %pad_maximum_fusion.q_ref, bf16[16,128,256]{2,1,0:T(8,128)(2,1)S(1)} %constant_dynamic-update-slice_fusion.mine, ...), custom_call_target="tpu_custom_call" | custom-call | flops 4831838208 | bytes 9000000 | tf_op jit(solution)/shard_map/attend_next/pallas_call | solution.py:297
  118.4 1.3 copy-done.7
  119.6 11.6 %attend_last.1 = (bf16[576,128]{1,0:T(8,128)(2,1)S(1)}, bf16[576,128]{1,0:T(8,128)(2,1)S(1)}, bf16[576,128]{1,0:T(8,128)(2,1)S(1)}, bf16[576,128]{1,0:T(8,128)(2,1)S(1)}) custom-call(s32[4]{0:T(128)S(1)} %pad_add_fusion.place, s32[32,32]{1,0:T(8,128)S(1)} %copy-done.6, bf16[4,576,128]{2,1,0:T(8,128)(2,1)S(1)} %pad_maximum_fusion.q_ref, ...), custom_call_target="tpu_custom_call" | custom-call | flops 2415919104 | bytes 6000000 | tf_op jit(solution)/shard_map/attend_last/pallas_call | solution.py:306
  131.2 4.3 %collective-permute-start.12 = (bf16[576,128]{1,0:T(8,128)(2,1)S(1)}, bf16[576,128]{1,0:T(8,128)(2,1)S(1)}, u32[]{:S(2)}, u32[]{:S(2)}) collective-permute-start(bf16[576,128]{1,0:T(8,128)(2,1)S(1)} %get-tuple-element.27), channel_id=1, source_target_pairs={{0,12},{1,13},{2,14},{3,15},{4,0},{5,1},{6,2},{7,3},{8,4},{9,5},{1... | collective-permute-start | bytes 442376 | tf_op jit(solution)/shard_map/ppermute | solution.py:316
  135.5 6.1 %collective-permute-start.13 = (bf16[576,128]{1,0:T(8,128)(2,1)S(1)}, bf16[576,128]{1,0:T(8,128)(2,1)S(1)}, u32[]{:S(2)}, u32[]{:S(2)}) collective-permute-start(bf16[576,128]{1,0:T(8,128)(2,1)S(1)} %get-tuple-element.28), channel_id=1, source_target_pairs={{0,8},{1,9},{2,10},{3,11},{4,12},{5,13},{6,14},{7,15},{8,0},{9,1},... | collective-permute-start | bytes 442376 | tf_op jit(solution)/shard_map/ppermute | solution.py:316
  141.7 1.9 %collective-permute-start.14 = (bf16[576,128]{1,0:T(8,128)(2,1)S(1)}, bf16[576,128]{1,0:T(8,128)(2,1)S(1)}, u32[]{:S(2)}, u32[]{:S(2)}) collective-permute-start(bf16[576,128]{1,0:T(8,128)(2,1)S(1)} %get-tuple-element.29), channel_id=1, source_target_pairs={{0,4},{1,5},{2,6},{3,7},{4,8},{5,9},{6,10},{7,11},{8,12},{9,13},{1... | collective-permute-start | bytes 442376 | tf_op jit(solution)/shard_map/ppermute | solution.py:316
  143.6 10.0 %collective-permute-done.13.r2 = bf16[576,128]{1,0:T(8,128)(2,1)S(1)} collective-permute-done((bf16[576,128]{1,0:T(8,128)(2,1)S(1)}, bf16[576,128]{1,0:T(8,128)(2,1)S(1)}, u32[]{:S(2)}, u32[]{:S(2)}) %collective-permute-start.13) | collective-permute-done | bytes 147488 | tf_op jit(solution)/shard_map/ppermute | solution.py:316
  153.6 7.4 %collective-permute-done.14.r3 = bf16[576,128]{1,0:T(8,128)(2,1)S(1)} collective-permute-done((bf16[576,128]{1,0:T(8,128)(2,1)S(1)}, bf16[576,128]{1,0:T(8,128)(2,1)S(1)}, u32[]{:S(2)}, u32[]{:S(2)}) %collective-permute-start.14) | collective-permute-done | bytes 147488 | tf_op jit(solution)/shard_map/ppermute | solution.py:316
  161.0 1.5 unpack_outputs.1
  (42 shorter events, 1.2 us)
Async XLA Ops:
  0.6 18.0 %copy-start.2 = (bf16[128,512]{1,0:T(8,128)(2,1)S(1)}, bf16[128,512]{1,0:T(8,128)(2,1)}, u32[]{:S(2)}) copy-start(bf16[128,512]{1,0:T(8,128)(2,1)} %v_ref.2) | copy-start | bytes 393220
  0.6 18.0 %copy-start.3 = (bf16[16,2048]{1,0:T(8,128)(2,1)S(1)}, bf16[16,2048]{1,0:T(8,128)(2,1)}, u32[]{:S(2)}) copy-start(bf16[16,2048]{1,0:T(8,128)(2,1)} %bq_ref.1) | copy-start | bytes 196612
  0.7 18.0 %copy-start = (bf16[128,2048]{1,0:T(8,128)(2,1)S(1)}, bf16[128,2048]{1,0:T(8,128)(2,1)}, u32[]{:S(2)}) copy-start(bf16[128,2048]{1,0:T(8,128)(2,1)} %q_ref.1) | copy-start | bytes 1572868
  0.7 18.0 %copy-start.1 = (bf16[128,512]{1,0:T(8,128)(2,1)S(1)}, bf16[128,512]{1,0:T(8,128)(2,1)}, u32[]{:S(2)}) copy-start(bf16[128,512]{1,0:T(8,128)(2,1)} %k_ref.2) | copy-start | bytes 393220
  0.7 0.8 copy-start.4
  1.5 0.7 copy-start.5
  3.0 37.4 %all-to-all-start = ((bf16[64,16,256]{2,1,0:T(8,128)(2,1)}), bf16[64,16,256]{2,1,0:T(8,128)(2,1)S(1)}, u32[]{:S(2)}, u32[]{:S(2)}) async-start(bf16[64,16,256]{2,1,0:T(8,128)(2,1)} %pack_beacons.1), calls=%async_computation | async-start | bytes 1048576 | tf_op jit(solution)/shard_map/all_to_all | solution.py:257
  19.4 21.1 %collective-permute-start.2 = (bf16[832,128]{1,0:T(8,128)(2,1)S(1)}, bf16[832,128]{1,0:T(8,128)(2,1)S(1)}, u32[]{:S(2)}, u32[]{:S(2)}) collective-permute-start(bf16[832,128]{1,0:T(8,128)(2,1)S(1)} %get-tuple-element.19), channel_id=1, source_target_pairs={{0,12},{1,13},{2,14},{3,15},{4,0},{5,1},{6,2},{7,3},{8,4},{9,5},{1... | collective-permute-start | bytes 638984 | tf_op jit(solution)/shard_map/ppermute | solution.py:268
  24.0 28.9 %collective-permute-start.1 = (bf16[832,128]{1,0:T(8,128)(2,1)S(1)}, bf16[832,128]{1,0:T(8,128)(2,1)S(1)}, u32[]{:S(2)}, u32[]{:S(2)}) collective-permute-start(bf16[832,128]{1,0:T(8,128)(2,1)S(1)} %get-tuple-element.18), channel_id=1, source_target_pairs={{0,8},{1,9},{2,10},{3,11},{4,12},{5,13},{6,14},{7,15},{8,0},{9,1},... | collective-permute-start | bytes 638984 | tf_op jit(solution)/shard_map/ppermute | solution.py:268
  29.2 23.8 %collective-permute-start = (bf16[832,128]{1,0:T(8,128)(2,1)S(1)}, bf16[832,128]{1,0:T(8,128)(2,1)S(1)}, u32[]{:S(2)}, u32[]{:S(2)}) collective-permute-start(bf16[832,128]{1,0:T(8,128)(2,1)S(1)} %get-tuple-element.17), channel_id=1, source_target_pairs={{0,4},{1,5},{2,6},{3,7},{4,8},{5,9},{6,10},{7,11},{8,12},{9,13},{1... | collective-permute-start | bytes 638984 | tf_op jit(solution)/shard_map/ppermute | solution.py:268
  40.5 16.4 %collective-permute-start.5 = (bf16[8,128,256]{2,1,0:T(8,128)(2,1)S(1)}, bf16[8,128,256]{2,1,0:T(8,128)(2,1)S(1)}, u32[]{:S(2)}, u32[]{:S(2)}) collective-permute-start(bf16[8,128,256]{2,1,0:T(8,128)(2,1)S(1)} %bitcast.21), channel_id=1, source_target_pairs={{0,128},{1,129},{2,130},{3,131},{4,132},{5,133},{6,134},{7,135},{8... | collective-permute-start | bytes 1572872 | tf_op jit(solution)/shard_map/ppermute | solution.py:276
  41.8 16.4 %collective-permute-start.6 = (bf16[8,128,256]{2,1,0:T(8,128)(2,1)S(1)}, bf16[8,128,256]{2,1,0:T(8,128)(2,1)S(1)}, u32[]{:S(2)}, u32[]{:S(2)}) collective-permute-start(bf16[8,128,256]{2,1,0:T(8,128)(2,1)S(1)} %bitcast.22), channel_id=1, source_target_pairs={{0,384},{1,385},{2,386},{3,387},{4,388},{5,389},{6,390},{7,391},{8... | collective-permute-start | bytes 1572872 | tf_op jit(solution)/shard_map/ppermute | solution.py:277
  53.0 10.9 %collective-permute-start.9 = (bf16[4,256,128]{2,1,0:T(8,128)(2,1)S(1)}, bf16[4,256,128]{2,1,0:T(8,128)(2,1)S(1)}, u32[]{:S(2)}, u32[]{:S(2)}) collective-permute-start(bf16[4,256,128]{2,1,0:T(8,128)(2,1)S(1)} %pad_maximum_fusion.1.kv_o), channel_id=1, source_target_pairs={{0,2},{1,3},{2,0},{3,1},{4,6},{5,7},{6,4},{7,5},{8,10},{9,11},{10,... | collective-permute-start | bytes 786440 | tf_op jit(solution)/shard_map/ppermute | solution.py:272
  54.9 26.8 %collective-permute-start.8 = (bf16[4,256,128]{2,1,0:T(8,128)(2,1)S(1)}, bf16[4,256,128]{2,1,0:T(8,128)(2,1)S(1)}, u32[]{:S(2)}, u32[]{:S(2)}) collective-permute-start(bf16[4,256,128]{2,1,0:T(8,128)(2,1)S(1)} %pad_maximum_fusion.1.kv_o), channel_id=1, source_target_pairs={{0,1},{1,0},{2,3},{3,2},{4,5},{5,4},{6,7},{7,6},{8,9},{9,8},{10,11... | collective-permute-start | bytes 786440 | tf_op jit(solution)/shard_map/ppermute | solution.py:273
  58.2 23.6 %copy-start.10 = (s32[256]{0:T(256)S(1)}, s32[256]{0:T(256)}, u32[]{:S(2)}) copy-start(s32[256]{0:T(256)} %param.14) | copy-start | bytes 3076
  58.2 23.7 %copy-start.6 = (s32[32,32]{1,0:T(8,128)S(1)}, s32[32,32]{1,0:T(8,128)}, u32[]{:S(2)}) copy-start(s32[32,32]{1,0:T(8,128)} %visible.5) | copy-start | bytes 12292
  58.2 42.9 %collective-permute-start.7 = (bf16[16,128,256]{2,1,0:T(8,128)(2,1)S(1)}, bf16[16,128,256]{2,1,0:T(8,128)(2,1)S(1)}, u32[]{:S(2)}, u32[]{:S(2)}) collective-permute-start(bf16[16,128,256]{2,1,0:T(8,128)(2,1)S(1)} %constant_dynamic-update-slice_fusion.mine), channel_id=1, source_target_pairs={{0,1},{1,0},{2,3},{3,2},{4,5},{5,4},{6,7},{7,6},{8,9},{9,8},{10,11... | collective-permute-start | bytes 3145736 | tf_op jit(solution)/shard_map/ppermute | solution.py:281
  60.2 21.6 %collective-permute-start.11 = (bf16[8,128,256]{2,1,0:T(8,128)(2,1)S(1)}, bf16[8,128,256]{2,1,0:T(8,128)(2,1)S(1)}, u32[]{:S(2)}, u32[]{:S(2)}) collective-permute-start(bf16[8,128,256]{2,1,0:T(8,128)(2,1)S(1)} %bitcast.23), channel_id=1, source_target_pairs={{0,1},{1,0},{2,3},{3,2},{4,5},{5,4},{6,7},{7,6},{8,9},{9,8},{10,11... | collective-permute-start | bytes 1572872 | tf_op jit(solution)/shard_map/ppermute | solution.py:279
  62.6 17.2 %collective-permute-start.3 = (bf16[8,128,256]{2,1,0:T(8,128)(2,1)S(1)}, bf16[8,128,256]{2,1,0:T(8,128)(2,1)S(1)}, u32[]{:S(2)}, u32[]{:S(2)}) collective-permute-start(bf16[8,128,256]{2,1,0:T(8,128)(2,1)S(1)} %bitcast.24), channel_id=1, source_target_pairs={{0,256},{1,257},{2,258},{3,259},{4,260},{5,261},{6,262},{7,263},{8... | collective-permute-start | bytes 1572872 | tf_op jit(solution)/shard_map/ppermute | solution.py:278
  63.9 17.8 %collective-permute-start.10 = (bf16[4,256,128]{2,1,0:T(8,128)(2,1)S(1)}, bf16[4,256,128]{2,1,0:T(8,128)(2,1)S(1)}, u32[]{:S(2)}, u32[]{:S(2)}) collective-permute-start(bf16[4,256,128]{2,1,0:T(8,128)(2,1)S(1)} %collective-permute-done.9.kv_z), channel_id=1, source_target_pairs={{0,1},{1,0},{2,3},{3,2},{4,5},{5,4},{6,7},{7,6},{8,9},{9,8},{10,11... | collective-permute-start | bytes 786440 | tf_op jit(solution)/shard_map/ppermute | solution.py:274
  79.8 38.5 %collective-permute-start.4 = (bf16[8,128,256]{2,1,0:T(8,128)(2,1)S(1)}, bf16[8,128,256]{2,1,0:T(8,128)(2,1)S(1)}, u32[]{:S(2)}, u32[]{:S(2)}) collective-permute-start(bf16[8,128,256]{2,1,0:T(8,128)(2,1)S(1)} %collective-permute-done.3.mine), channel_id=1, source_target_pairs={{0,1},{1,0},{2,3},{3,2},{4,5},{5,4},{6,7},{7,6},{8,9},{9,8},{10,11... | collective-permute-start | bytes 1572872 | tf_op jit(solution)/shard_map/ppermute | solution.py:282
  99.0 1.0 copy-start.8
  100.1 1.0 copy-start.9
  118.3 1.3 copy-start.7
  131.2 12.4 %collective-permute-start.12 = (bf16[576,128]{1,0:T(8,128)(2,1)S(1)}, bf16[576,128]{1,0:T(8,128)(2,1)S(1)}, u32[]{:S(2)}, u32[]{:S(2)}) collective-permute-start(bf16[576,128]{1,0:T(8,128)(2,1)S(1)} %get-tuple-element.27), channel_id=1, source_target_pairs={{0,12},{1,13},{2,14},{3,15},{4,0},{5,1},{6,2},{7,3},{8,4},{9,5},{1... | collective-permute-start | bytes 442376 | tf_op jit(solution)/shard_map/ppermute | solution.py:316
  135.5 18.1 %collective-permute-start.13 = (bf16[576,128]{1,0:T(8,128)(2,1)S(1)}, bf16[576,128]{1,0:T(8,128)(2,1)S(1)}, u32[]{:S(2)}, u32[]{:S(2)}) collective-permute-start(bf16[576,128]{1,0:T(8,128)(2,1)S(1)} %get-tuple-element.28), channel_id=1, source_target_pairs={{0,8},{1,9},{2,10},{3,11},{4,12},{5,13},{6,14},{7,15},{8,0},{9,1},... | collective-permute-start | bytes 442376 | tf_op jit(solution)/shard_map/ppermute | solution.py:316
  141.7 19.3 %collective-permute-start.14 = (bf16[576,128]{1,0:T(8,128)(2,1)S(1)}, bf16[576,128]{1,0:T(8,128)(2,1)S(1)}, u32[]{:S(2)}, u32[]{:S(2)}) collective-permute-start(bf16[576,128]{1,0:T(8,128)(2,1)S(1)} %get-tuple-element.29), channel_id=1, source_target_pairs={{0,4},{1,5},{2,6},{3,7},{4,8},{5,9},{6,10},{7,11},{8,12},{9,13},{1... | collective-permute-start | bytes 442376 | tf_op jit(solution)/shard_map/ppermute | solution.py:316
